TPU v7x, 32 devices: a whole 2x2x4 slice. The times are simulated.
32 devices in a mesh: hyper: 2 (over y), row: 16 (over z, x, core).
Axes of the slice: x: 2, y: 2, z: 4, core: 2. Of those that a mesh axis runs over, the one named last changes fastest.
Arguments:
- top_sigma: bfloat16 [20480, 10240], P(('hyper', 'row')), parts along dimension 0, may hold values from -1 to 5
- parent_pattern: int32 [16, 4], replicated, may hold values from 0 to 39, as said below
- parent_panel: bfloat16 [32, 1024, 256], P(('hyper', 'row')), parts along dimension 0, may hold values from -0.375 to 0.375
- parent_inverse: bfloat16 [32, 256, 256], P(('hyper', 'row')), parts along dimension 0, may hold values from -1 to 5
- child_pattern: int32 [128, 2], P('row'), may hold values from 0 to 3, as said below
- child_panel: bfloat16 [256, 768, 256], P(('hyper', 'row')), parts along dimension 0, may hold values from -0.375 to 0.375
- child_inverse: bfloat16 [256, 256, 256], P(('hyper', 'row')), parts along dimension 0, may hold values from -1 to 5
- child_count: int32 [16], P('row'), may hold values from 1 to 8
Outputs:
- parent_column: bfloat16 [32, 1024, 256], P(('hyper', 'row')), parts along dimension 0
- parent_block: float32 [32, 256, 256], P(('hyper', 'row')), parts along dimension 0
- child_column: bfloat16 [256, 768, 256], P(('hyper', 'row')), parts along dimension 0
- child_block: float32 [256, 256, 256], P(('hyper', 'row')), parts along dimension 0
There are 2 independent parts, one for each index of `hyper`. A program takes and returns all parts, laid end to end along the dimension named above; an argument that names none is the same for every part. Nothing has to cross between parts.
Inputs may be any that keep to these rules, and one draw needn't show every extreme that they name: `parent_pattern`: each row names 4 distinct supernodes in increasing order. `child_pattern`: each row names 2 distinct positions in increasing order.
All inputs are finite; a program needn't handle non-finite values.
Results may differ from a plain program's by a relative error of at most 0.005.
Values may be sent and summed in bfloat16 or wider, within the bound.
A program may use at most 192 MiB of HBM per device.

v0:
```python
import functools
import math

import jax
import jax.numpy as jnp
from jax import lax
from jax.experimental import pallas as pl
from jax.experimental.pallas import tpu as pltpu
from jax.sharding import PartitionSpec as P

BF16 = jnp.bfloat16
F32 = jnp.float32
VMEM_LIMIT = 40 * 2**20


def swapped(value, axis, distance):
    mask = 2**distance
    pairs = [(source, source ^ mask) for source in range(lax.axis_size(axis))]
    return lax.ppermute(value, axis, pairs)


def dot(a, b):
    return jnp.dot(a, b, preferred_element_type=F32)


def dot_t(a, b):
    return lax.dot_general(a, b, (((0,), (0,)), ((), ())), preferred_element_type=F32)


def from_top(per_parent, struct, super_, groups, cores, half, item, place, slot, pattern, top, out, sem):
    parent = item // per_parent
    row = (place[item] * cores + half) * groups
    for c in range(struct):
        column = pl.multiple_of(pattern[parent, c] * super_, super_)
        yield pltpu.make_async_copy(
            top.at[pl.ds(row, groups), :, pl.ds(column, super_)],
            out.at[:, c, slot[item]],
            sem,
        )


def give_kernel(items, sizes, core, place, slot, pattern, top, out, sem):
    def each(act):
        @pl.loop(0, items)
        def _(item):
            @pl.when(place[item] >= 0)
            def _():
                for copy in from_top(*sizes, 1 - core[0], item, place, slot, pattern, top, out, sem):
                    act(copy)

    each(lambda copy: copy.start())
    each(lambda copy: copy.wait())


def pack_kernel(items, sizes, core, place, slot, pattern, top, got, out, sem):
    def each(act):
        @pl.loop(0, items)
        def _(item):
            @pl.when(place[item] >= 0)
            def _():
                for copy in from_top(*sizes, core[0], item, place, slot, pattern, top, out, sem):
                    act(copy)

            @pl.when(place[item] == -1)
            def _():
                act(pltpu.make_async_copy(got.at[:, :, slot[item]], out.at[:, :, slot[item]], sem))

    each(lambda copy: copy.start())
    each(lambda copy: copy.wait())


def pick_kernel(items, per_parent, cores, chip, slot, held, out, sem):
    @pl.loop(0, items)
    def _(item):
        for core in range(cores):
            pltpu.make_async_copy(
                held.at[chip[item] * cores + core, slot[item]],
                out.at[item // per_parent, lax.rem(item, per_parent), core],
                sem,
            ).start()

    pltpu.make_async_copy(out, out, sem).wait()


def sigma_block(raw, a, c):
    groups, _, _, halves = raw.shape[:4]
    return jnp.concatenate(
        [raw[i, c, a, h] for h in range(halves) for i in range(groups)], axis=0
    )


def parent_kernel(raw, panel, inverse, column, diagonal, both):
    struct = raw.shape[1]
    width = inverse.shape[-1]
    total = inverse[0].astype(F32)
    for a in range(struct):
        product = jnp.zeros((width, width), F32)
        for c in range(struct):
            product += dot(sigma_block(raw, a, c), panel[0, pl.ds(c * width, width), :])
        col = (-product).astype(BF16)
        column[0, pl.ds(a * width, width), :] = col
        both[a] = col
        total -= dot_t(panel[0, pl.ds(a * width, width), :], col)
    diagonal[0] = total
    both[struct] = total.astype(BF16)


def child_kernel(positions, count, raw, both, panel, inverse, column, diagonal, sigma, beside_t):
    struct = raw.shape[1]
    width = inverse.shape[-1]
    picks = positions.shape[1]
    child = pl.program_id(0)

    @pl.when(child == 0)
    def _():
        for a in range(struct):
            for c in range(struct):
                sigma[a * struct + c] = sigma_block(raw, a, c)
            beside_t[a] = both[a].T

    @pl.when(child < count[0])
    def _():
        q = [positions[child, i] for i in range(picks)]
        parts = [panel[0, pl.ds(i * width, width), :] for i in range(picks + 1)]
        product = dot(both[struct], parts[0])
        for i in range(picks):
            product += dot(beside_t[q[i]], parts[1 + i])
        col = (-product).astype(BF16)
        column[0, pl.ds(0, width), :] = col
        total = inverse[0].astype(F32) - dot_t(parts[0], col)
        for i in range(picks):
            product = dot(both[q[i]], parts[0])
            for j in range(picks):
                product += dot(sigma[q[i] * struct + q[j]], parts[1 + j])
            col = (-product).astype(BF16)
            column[0, pl.ds((1 + i) * width, width), :] = col
            total -= dot_t(parts[1 + i], col)
        diagonal[0] = total

    @pl.when(child >= count[0])
    def _():
        column[...] = jnp.zeros_like(column)
        diagonal[...] = jnp.zeros_like(diagonal)


def parent_solve(raw, panel, inverse):
    struct, width = raw.shape[1], inverse.shape[-1]
    return pl.pallas_call(
        parent_kernel,
        out_shape=(
            jax.ShapeDtypeStruct((1, struct * width, width), BF16),
            jax.ShapeDtypeStruct((1, width, width), F32),
            jax.ShapeDtypeStruct((struct + 1, width, width), BF16),
        ),
        compiler_params=pltpu.CompilerParams(vmem_limit_bytes=VMEM_LIMIT),
        name="parent",
    )(raw, panel, inverse)


def children_solve(raw, both, positions, panel, inverse, count):
    kids, rows, width = panel.shape
    struct = raw.shape[1]

    def whole(shape):
        return pl.BlockSpec(shape, lambda k, *_: (0,) * len(shape))

    def one(shape):
        return pl.BlockSpec((1,) + shape, lambda k, *_: (k, 0, 0))

    return pl.pallas_call(
        child_kernel,
        grid_spec=pltpu.PrefetchScalarGridSpec(
            num_scalar_prefetch=2,
            grid=(kids,),
            in_specs=[whole(raw.shape), whole(both.shape), one((rows, width)), one((width, width))],
            out_specs=[one((rows, width)), one((width, width))],
            scratch_shapes=[
                pltpu.VMEM((struct * struct, width, width), BF16),
                pltpu.VMEM((struct, width, width), BF16),
            ],
        ),
        out_shape=(
            jax.ShapeDtypeStruct((kids, rows, width), BF16),
            jax.ShapeDtypeStruct((kids, width, width), F32),
        ),
        compiler_params=pltpu.CompilerParams(vmem_limit_bytes=VMEM_LIMIT),
        name="children",
    )(positions, count, raw, both, panel, inverse)


def exchange_plain(top_sigma, parent_pattern, width):
    devices = parent_pattern.shape[0]
    strip, total_rows = top_sigma.shape
    struct = parent_pattern.shape[1]
    blocks = total_rows // width
    picked = jnp.take(top_sigma.reshape(strip, blocks, width), parent_pattern, axis=1)
    outgoing = jnp.transpose(picked, (1, 0, 2, 3)).reshape(devices, strip, struct * width)
    arrived = lax.all_to_all(outgoing, "row", split_axis=0, concat_axis=1, tiled=True)
    columns = arrived[0].reshape(blocks, width, struct, width)
    mine = jnp.take(columns, parent_pattern[lax.axis_index("row")], axis=0)
    return jnp.transpose(mine, (2, 0, 1, 3))[None, :, :, None]


def schedule(parent_pattern, halves, own, cores):
    me = lax.axis_index("row")
    units = (parent_pattern[:, :, None] * halves + jnp.arange(halves, dtype=jnp.int32)).reshape(-1)
    chip = units // (own * cores)
    earlier = jnp.arange(units.size)[None, :] < jnp.arange(units.size)[:, None]
    slot = jnp.sum(
        jnp.logical_and(chip[None, :] == chip[:, None], earlier), axis=1, dtype=jnp.int32
    )
    offset = units - me * own
    mine = jnp.logical_and(offset >= 0, offset < own)
    place = jnp.where(mine, offset, jnp.where(chip == me // cores, -1, -2))
    return chip, place, slot


def exchange_two_hops(top_sigma, parent_pattern, width, unit, groups, cores):
    devices, struct = parent_pattern.shape
    halves, own = width // unit, top_sigma.shape[0] // unit
    per_parent = struct * halves
    items = devices * per_parent
    piece = unit // (groups * cores)
    chip, place, slot = schedule(parent_pattern, halves, own, cores)
    core = lax.rem(lax.axis_index("row"), cores).astype(jnp.int32)[None]
    most = devices * min(cores * own, per_parent)
    levels = [k for k in (18, 20, 21, 22, 23, 24, 25, 26, 28, 30, 33, 40, 56, 80) if k < most] + [most]
    strips = top_sigma.reshape(top_sigma.shape[0] // piece, piece, top_sigma.shape[1])
    smem = pl.BlockSpec(memory_space=pltpu.SMEM)
    hbm = pl.BlockSpec(memory_space=pl.ANY)
    vmem = pl.BlockSpec(memory_space=pltpu.VMEM)
    sizes = (per_parent, struct, width, groups, cores)
    params = pltpu.CompilerParams(vmem_limit_bytes=VMEM_LIMIT)

    def hop(slots, strips, core, chip, place, slot, pattern):
        shape = jax.ShapeDtypeStruct((groups, struct, slots, piece, width), BF16)
        give = pl.pallas_call(
            functools.partial(give_kernel, items, sizes),
            out_shape=shape,
            in_specs=[smem, smem, smem, smem, hbm],
            out_specs=vmem,
            scratch_shapes=[pltpu.SemaphoreType.DMA],
            compiler_params=params,
            name="give",
        )(core, place, slot, pattern, strips)
        got = swapped(give, "row", 0)
        outgoing = pl.pallas_call(
            functools.partial(pack_kernel, items, sizes),
            out_shape=shape,
            in_specs=[smem, smem, smem, smem, hbm, hbm],
            out_specs=vmem,
            scratch_shapes=[pltpu.SemaphoreType.DMA],
            compiler_params=params,
            name="pack",
        )(core, place, slot, pattern, strips, got)
        outgoing = outgoing.reshape(devices, slots, piece, width)
        held = lax.all_to_all(outgoing, "row", split_axis=0, concat_axis=0, tiled=True)
        return pl.pallas_call(
            functools.partial(pick_kernel, items, per_parent, cores),
            out_shape=jax.ShapeDtypeStruct((devices, per_parent, cores, piece, width), BF16),
            in_specs=[smem, smem, hbm],
            out_specs=hbm,
            scratch_shapes=[pltpu.SemaphoreType.DMA],
            name="pick",
        )(chip, slot, held)

    needed = jnp.max(slot) + 1
    level = jnp.sum(needed > jnp.array(levels[:-1], jnp.int32), dtype=jnp.int32)
    outgoing = lax.switch(
        level,
        [functools.partial(hop, slots) for slots in levels],
        strips, core, chip, place, slot, parent_pattern,
    )
    arrived = lax.all_to_all(outgoing, "row", split_axis=0, concat_axis=0, tiled=True)
    return arrived.reshape(groups, struct, struct, halves * cores, piece, width)


def local(
    top_sigma,
    parent_pattern,
    parent_panel,
    parent_inverse,
    child_pattern,
    child_panel,
    child_inverse,
    child_count,
):
    width = parent_inverse.shape[-1]
    devices, struct = parent_pattern.shape
    unit = math.gcd(width, top_sigma.shape[0])
    groups = devices // struct
    cores = 2
    if devices % (struct * cores) == 0 and unit % (16 * groups * cores) == 0:
        raw = exchange_two_hops(top_sigma, parent_pattern, width, unit, groups, cores)
    else:
        raw = exchange_plain(top_sigma, parent_pattern, width)
    other_raw = swapped(raw, "row", 0)
    column, diagonal, both = parent_solve(raw, parent_panel, parent_inverse)
    other_both = swapped(both, "row", 0)
    child_col, child_diag = children_solve(
        other_raw, other_both, child_pattern, child_panel, child_inverse, child_count
    )
    return (column, diagonal, child_col, child_diag)


def solution(mesh):
    in_specs = (
        P(("hyper", "row"), None),
        P(),
        P(("hyper", "row"), None, None),
        P(("hyper", "row"), None, None),
        P("row", None),
        P(("hyper", "row"), None, None),
        P(("hyper", "row"), None, None),
        P("row"),
    )
    out_specs = (
        P(("hyper", "row"), None, None),
        P(("hyper", "row"), None, None),
        P(("hyper", "row"), None, None),
        P(("hyper", "row"), None, None),
    )
    return jax.shard_map(local, mesh=mesh, in_specs=in_specs, out_specs=out_specs, check_vma=False)
```

profile of v0, /device:TPU:0, one launch (start us, length us, event | category | flops | bytes accessed | tf_op | source)
XLA Modules:
  0.0 188.8 jit_solution(858918641558459543)
XLA Ops:
  0.6 0.7 broadcast_multiply_fusion
  1.3 0.1 copy.47
  1.4 0.1 fusion.3
  1.5 0.1 fusion.2
  1.6 0.1 div.26
  1.8 0.1 sub.22
  1.9 0.1 and.28
  2.1 0.2 convert_reduce_fusion
  2.3 0.6 reduce_max.9
  3.6 1.3 fusion.4
  5.5 108.5 %conditional.1 = (bf16[16,8,2,16,256]{4,3,2,1,0:T(8,128)(2,1)S(1)}) conditional(s32[]{:T(128)} %clamp.3, (s32[1]{0:T(128)}, s32[128]{0:T(128)S(1)}, s32[128]{0:T(128)S(1)}, s32[16,4]{0,1:T(4,128)}, bf16[40,16,10240]{2,1,0:T(8,128)(2,1)}, /*index=5*/s32[128]{0:T(128)S(1)}) %tuple.117, (s32[1]{0:T(128)}, ...), branch_computations={%region_3.4_spmd, %region_4.5_spmd, %region_5.6_spmd, %region_6.7_... | conditional | bytes 139985536 | solution.py:269
  5.6 0.8 copy.55.pattern
  6.3 0.0 copy-start.11
  6.3 8.2 %give.22 = bf16[4,4,26,16,256]{4,3,2,1,0:T(8,128)(2,1)S(1)} custom-call(s32[1]{0:T(128)} %get-tuple-element.240.core, s32[128]{0:T(128)S(1)} %get-tuple-element.241.place, s32[128]{0:T(128)S(1)} %get-tuple-element.239.slot, s32[16,4]{1,0:T(8,128)S(1)} %copy.55.pattern, bf16[40,16,10240]{2,1,0:T(8,128)(2,1)} %get-tuple-element.243.top), custom_call_target="tpu_custom_call" | custom-call | tf_op jit(solution)/shard_map/cond/branch_7_fun/give/pallas_call | solution.py:237
  14.5 0.5 collective-permute-start.7
  15.0 5.7 %collective-permute-done.7.got = bf16[4,4,26,16,256]{4,3,2,1,0:T(8,128)(2,1)S(1)} collective-permute-done((bf16[4,4,26,16,256]{4,3,2,1,0:T(8,128)(2,1)S(1)}, bf16[4,4,26,16,256]{4,3,2,1,0:T(8,128)(2,1)S(1)}, u32[]{:S(2)}, u32[]{:S(2)}) %collective-permute-start.7) | collective-permute-done | bytes 3407904 | tf_op jit(solution)/shard_map/cond/branch_7_fun/ppermute | solution.py:19
  20.7 0.0 copy-done.11
  20.7 5.6 %pack.22 = bf16[4,4,26,16,256]{4,3,2,1,0:T(8,128)(2,1)S(1)} custom-call(s32[1]{0:T(128)} %get-tuple-element.240.core, s32[128]{0:T(128)S(1)} %get-tuple-element.241.place, s32[128]{0:T(128)S(1)} %get-tuple-element.239.slot, s32[16,4]{1,0:T(8,128)S(1)} %copy.55.pattern, bf16[40,16,10240]{2,1,0:T(8,128)(2,1)S(1)} %copy-done.11, ...), custom_call_target="tpu_custom_call" | custom-call | tf_op jit(solution)/shard_map/cond/branch_7_fun/pack/pallas_call | solution.py:247
  26.3 84.5 %all_to_all.72.held = bf16[16,26,16,256]{3,2,1,0:T(8,128)(2,1)} all-to-all(bf16[16,26,16,256]{3,2,1,0:T(8,128)(2,1)S(1)} %bitcast.24), channel_id=1, replica_groups=mesh['hyper'=2,'row'=16] {'row'}, dimensions={0} | all-to-all | bytes 6815744 | tf_op jit(solution)/shard_map/cond/branch_7_fun/all_to_all | solution.py:257
  110.7 3.2 %pick.22 = bf16[16,8,2,16,256]{4,3,2,1,0:T(8,128)(2,1)S(1)} custom-call(s32[128]{0:T(128)S(1)} %get-tuple-element.238.chip, s32[128]{0:T(128)S(1)} %get-tuple-element.239.slot, bf16[16,26,16,256]{3,2,1,0:T(8,128)(2,1)} %all_to_all.72.held), custom_call_target="tpu_custom_call" | custom-call | tf_op jit(solution)/shard_map/cond/branch_7_fun/pick/pallas_call | solution.py:258
  114.0 0.0 copy-start.16
  114.0 1.3 copy-done.16
  115.3 0.0 copy-start.3
  115.3 0.0 copy-start.2
  115.3 0.0 copy-start.17
  115.3 0.0 copy-start.1
  115.3 51.6 %all_to_all.80 = bf16[16,8,2,16,256]{4,3,2,1,0:T(8,128)(2,1)S(1)} all-to-all(bf16[16,8,2,16,256]{4,3,2,1,0:T(8,128)(2,1)} %copy-done.16), channel_id=1, replica_groups=mesh['hyper'=2,'row'=16] {'row'}, dimensions={0} | all-to-all | bytes 4194304 | tf_op jit(solution)/shard_map/all_to_all | solution.py:274
  167.0 0.8 collective-permute-start.15
  167.7 0.0 copy-done.3
  167.7 0.0 copy-done.2
  167.7 2.9 %parent.1 = (bf16[1,1024,256]{2,1,0:T(8,128)(2,1)}, f32[1,256,256]{2,1,0:T(8,128)}, bf16[5,256,256]{2,1,0:T(8,128)(2,1)}) custom-call(bf16[4,4,4,4,16,256]{5,4,3,2,1,0:T(8,128)(2,1)S(1)} %bitcast.33, bf16[1,1024,256]{2,1,0:T(8,128)(2,1)S(1)} %copy-done.2, bf16[1,256,256]{2,1,0:T(8,128)(2,1)S(1)} %copy-done.3), custom_call_target="tpu_custom_call" | custom-call | tf_op jit(solution)/shard_map/parent/pallas_call | solution.py:148
  170.6 0.0 collective-permute-start.16
  170.6 0.0 copy-done.17
  170.6 0.1 copy.63.positions
  171.4 1.7 collective-permute-done.16.both
  173.1 0.0 collective-permute-done.15.raw
  173.1 0.0 copy-done.1
  173.1 0.0 copy-start
  173.1 1.9 copy-done
  175.0 13.8 %children.1 = (bf16[8,768,256]{2,1,0:T(8,128)(2,1)}, f32[8,256,256]{2,1,0:T(8,128)}) custom-call(s32[8,2]{1,0:T(8,128)S(1)} %copy.63.positions, s32[1]{0:T(128)S(6)} %copy.79.count, bf16[4,4,4,4,16,256]{5,4,3,2,1,0:T(8,128)(2,1)} %collective-permute-done.15.raw, bf16[5,256,256]{2,1,0:T(8,128)(2,1)} %collective-permute-done.16.both, ...), custom_call_target="tpu_custom_call" | custom-call | tf_op jit(solution)/shard_map/children/pallas_call | solution.py:170
  (1 shorter events, 0.0 us)
Async XLA Ops:
  6.3 14.4 %copy-start.11 = (bf16[40,16,10240]{2,1,0:T(8,128)(2,1)S(1)}, bf16[40,16,10240]{2,1,0:T(8,128)(2,1)}, u32[]{:S(2)}) copy-start(bf16[40,16,10240]{2,1,0:T(8,128)(2,1)} %get-tuple-element.243.top) | copy-start | bytes 39321604 | tf_op jit(solution)/shard_map/cond
  14.5 6.2 %collective-permute-start.7 = (bf16[4,4,26,16,256]{4,3,2,1,0:T(8,128)(2,1)S(1)}, bf16[4,4,26,16,256]{4,3,2,1,0:T(8,128)(2,1)S(1)}, u32[]{:S(2)}, u32[]{:S(2)}) collective-permute-start(bf16[4,4,26,16,256]{4,3,2,1,0:T(8,128)(2,1)S(1)} %give.22), channel_id=1, source_target_pairs={{0,1},{1,0},{2,3},{3,2},{4,5},{5,4},{6,7},{7,6},{8,9},{9,8},{10,11... | collective-permute-start | bytes 10223624 | tf_op jit(solution)/shard_map/cond/branch_7_fun/ppermute | solution.py:19
  114.0 1.3 copy-start.16
  115.3 52.4 %copy-start.3 = (bf16[1,256,256]{2,1,0:T(8,128)(2,1)S(1)}, bf16[1,256,256]{2,1,0:T(8,128)(2,1)}, u32[]{:S(2)}) copy-start(bf16[1,256,256]{2,1,0:T(8,128)(2,1)} %inverse.2) | copy-start | bytes 393220
  115.3 52.4 %copy-start.2 = (bf16[1,1024,256]{2,1,0:T(8,128)(2,1)S(1)}, bf16[1,1024,256]{2,1,0:T(8,128)(2,1)}, u32[]{:S(2)}) copy-start(bf16[1,1024,256]{2,1,0:T(8,128)(2,1)} %panel.2) | copy-start | bytes 1572868
  115.3 55.3 %copy-start.17 = (s32[8,2]{0,1:T(2,128)S(1)}, s32[8,2]{0,1:T(2,128)}, u32[]{:S(2)}) copy-start(s32[8,2]{0,1:T(2,128)} %param.28) | copy-start | bytes 196
  115.3 57.8 %copy-start.1 = (bf16[8,256,256]{2,1,0:T(8,128)(2,1)S(1)}, bf16[8,256,256]{2,1,0:T(8,128)(2,1)}, u32[]{:S(2)}) copy-start(bf16[8,256,256]{2,1,0:T(8,128)(2,1)} %inverse.3) | copy-start | bytes 3145732
  167.0 6.1 %collective-permute-start.15 = (bf16[4,4,4,4,16,256]{5,4,3,2,1,0:T(8,128)(2,1)S(1)}, bf16[4,4,4,4,16,256]{5,4,3,2,1,0:T(8,128)(2,1)}, u32[]{:S(2)}, u32[]{:S(2)}) collective-permute-start(bf16[4,4,4,4,16,256]{5,4,3,2,1,0:T(8,128)(2,1)S(1)} %bitcast.32), channel_id=1, source_target_pairs={{0,1},{1,0},{2,3},{3,2},{4,5},{5,4},{6,7},{7,6},{8,9},{9,8},{10,11... | collective-permute-start | bytes 6291464 | tf_op jit(solution)/shard_map/ppermute | solution.py:19
  170.6 2.4 %collective-permute-start.16 = (bf16[5,256,256]{2,1,0:T(8,128)(2,1)}, bf16[5,256,256]{2,1,0:T(8,128)(2,1)}, u32[]{:S(2)}, u32[]{:S(2)}) collective-permute-start(bf16[5,256,256]{2,1,0:T(8,128)(2,1)} %get-tuple-element.297), channel_id=1, source_target_pairs={{0,1},{1,0},{2,3},{3,2},{4,5},{5,4},{6,7},{7,6},{8,9},{9,8},{10,11... | collective-permute-start | bytes 1966088 | tf_op jit(solution)/shard_map/ppermute | solution.py:19
  173.1 1.9 %copy-start = (bf16[8,768,256]{2,1,0:T(8,128)(2,1)S(1)}, bf16[8,768,256]{2,1,0:T(8,128)(2,1)}, u32[]{:S(2)}) copy-start(bf16[8,768,256]{2,1,0:T(8,128)(2,1)} %panel.3) | copy-start | bytes 9437188
where the time goes:
time: 189 us
  blocking collectives  136 us (72%)
  Pallas kernels  33.7 us (18%)
  waiting for transfers between devices  7.36 us (4%)
  local copies, waits for them, and re-layouts  4.58 us (2%)
  other arithmetic  3.01 us (2%)
  between operations  2.67 us (1%)
    all_to_all x1, blocking collectives, hop(): lax.all_to_all(outgoing, 'row', split_axis=0, concat_axis=0, tiled=True)  84.5 us
    all_to_all x1, blocking collectives, exchange_two_hops(): lax.all_to_all(outgoing, 'row', split_axis=0, concat_axis=0, tiled=True)  51.6 us
    pallas_call x1, Pallas kernels, children_solve(): pl.pallas_call(child_kernel, grid_spec=pltpu.PrefetchScalarGridSpec(num_s...  13.8 us
    pallas_call x1, Pallas kernels, hop(): pl.pallas_call(functools.partial(give_kernel, items, sizes), out_shape=sh...  8.16 us
    ppermute x3, waiting for transfers between devices, swapped(): return lax.ppermute(value, axis, pairs)  7.36 us
    pallas_call x1, Pallas kernels, hop(): pl.pallas_call(functools.partial(pack_kernel, items, sizes), out_shape=sh...  5.58 us
  transfers between devices with their start and end apart: 3, of which 2 were waited for; matrix products, arithmetic and copies ran while one was open for 0% of the time, Pallas kernels for 2%

commit v1 on v0

--- a/solution.py
+++ b/solution.py
@@ -39,34 +39,36 @@
         )
 
 
-def give_kernel(items, sizes, core, place, slot, pattern, top, out, sem):
-    def each(act):
-        @pl.loop(0, items)
-        def _(item):
-            @pl.when(place[item] >= 0)
-            def _():
-                for copy in from_top(*sizes, 1 - core[0], item, place, slot, pattern, top, out, sem):
-                    act(copy)
-
-    each(lambda copy: copy.start())
-    each(lambda copy: copy.wait())
-
-
-def pack_kernel(items, sizes, core, place, slot, pattern, top, got, out, sem):
-    def each(act):
-        @pl.loop(0, items)
-        def _(item):
-            @pl.when(place[item] >= 0)
-            def _():
-                for copy in from_top(*sizes, core[0], item, place, slot, pattern, top, out, sem):
-                    act(copy)
-
-            @pl.when(place[item] == -1)
-            def _():
-                act(pltpu.make_async_copy(got.at[:, :, slot[item]], out.at[:, :, slot[item]], sem))
-
-    each(lambda copy: copy.start())
-    each(lambda copy: copy.wait())
+def wait_units(number, out, sem):
+    @pl.loop(0, number)
+    def _(_):
+        pltpu.make_async_copy(out.at[:, :, 0], out.at[:, :, 0], sem).wait()
+
+
+def give_kernel(items, sizes, core, numbers, place, slot, pattern, top, out, sem):
+    @pl.loop(0, items)
+    def _(item):
+        @pl.when(place[item] >= 0)
+        def _():
+            for copy in from_top(*sizes, 1 - core[0], item, place, slot, pattern, top, out, sem):
+                copy.start()
+
+    wait_units(numbers[0], out, sem)
+
+
+def pack_kernel(items, sizes, core, numbers, place, slot, pattern, top, got, out, sem):
+    @pl.loop(0, items)
+    def _(item):
+        @pl.when(place[item] >= 0)
+        def _():
+            for copy in from_top(*sizes, core[0], item, place, slot, pattern, top, out, sem):
+                copy.start()
+
+        @pl.when(place[item] == -1)
+        def _():
+            pltpu.make_async_copy(got.at[:, :, slot[item]], out.at[:, :, slot[item]], sem).start()
+
+    wait_units(numbers[1], out, sem)
 
 
 def pick_kernel(items, per_parent, cores, chip, slot, held, out, sem):
@@ -105,7 +107,7 @@
     both[struct] = total.astype(BF16)
 
 
-def child_kernel(positions, count, raw, both, panel, inverse, column, diagonal, sigma, beside_t):
+def child_kernel(positions, count, raw, both, panel, inverse, column, diagonal, sigma, beside_t, matrix):
     struct = raw.shape[1]
     width = inverse.shape[-1]
     picks = positions.shape[1]
@@ -117,25 +119,20 @@
             for c in range(struct):
                 sigma[a * struct + c] = sigma_block(raw, a, c)
             beside_t[a] = both[a].T
+        matrix[pl.ds(0, width), pl.ds(0, width)] = both[struct]
 
     @pl.when(child < count[0])
     def _():
         q = [positions[child, i] for i in range(picks)]
-        parts = [panel[0, pl.ds(i * width, width), :] for i in range(picks + 1)]
-        product = dot(both[struct], parts[0])
+        at = [pl.ds((1 + i) * width, width) for i in range(picks)]
         for i in range(picks):
-            product += dot(beside_t[q[i]], parts[1 + i])
-        col = (-product).astype(BF16)
-        column[0, pl.ds(0, width), :] = col
-        total = inverse[0].astype(F32) - dot_t(parts[0], col)
-        for i in range(picks):
-            product = dot(both[q[i]], parts[0])
+            matrix[pl.ds(0, width), at[i]] = beside_t[q[i]]
+            matrix[at[i], pl.ds(0, width)] = both[q[i]]
             for j in range(picks):
-                product += dot(sigma[q[i] * struct + q[j]], parts[1 + j])
-            col = (-product).astype(BF16)
-            column[0, pl.ds((1 + i) * width, width), :] = col
-            total -= dot_t(parts[1 + i], col)
-        diagonal[0] = total
+                matrix[at[i], at[j]] = sigma[q[i] * struct + q[j]]
+        col = (-dot(matrix[...], panel[0])).astype(BF16)
+        column[0] = col
+        diagonal[0] = inverse[0].astype(F32) - dot_t(panel[0], col)
 
     @pl.when(child >= count[0])
     def _():
@@ -177,6 +174,7 @@
             scratch_shapes=[
                 pltpu.VMEM((struct * struct, width, width), BF16),
                 pltpu.VMEM((struct, width, width), BF16),
+                pltpu.VMEM((rows, rows), BF16),
             ],
         ),
         out_shape=(
@@ -223,6 +221,7 @@
     piece = unit // (groups * cores)
     chip, place, slot = schedule(parent_pattern, halves, own, cores)
     core = lax.rem(lax.axis_index("row"), cores).astype(jnp.int32)[None]
+    numbers = jnp.sum(place[None, :] >= jnp.array([[0], [-1]]), axis=1, dtype=jnp.int32)
     most = devices * min(cores * own, per_parent)
     levels = [k for k in (18, 20, 21, 22, 23, 24, 25, 26, 28, 30, 33, 40, 56, 80) if k < most] + [most]
     strips = top_sigma.reshape(top_sigma.shape[0] // piece, piece, top_sigma.shape[1])
@@ -232,27 +231,27 @@
     sizes = (per_parent, struct, width, groups, cores)
     params = pltpu.CompilerParams(vmem_limit_bytes=VMEM_LIMIT)
 
-    def hop(slots, strips, core, chip, place, slot, pattern):
+    def hop(slots, strips, core, numbers, chip, place, slot, pattern):
         shape = jax.ShapeDtypeStruct((groups, struct, slots, piece, width), BF16)
         give = pl.pallas_call(
             functools.partial(give_kernel, items, sizes),
             out_shape=shape,
-            in_specs=[smem, smem, smem, smem, hbm],
+            in_specs=[smem, smem, smem, smem, smem, hbm],
             out_specs=vmem,
             scratch_shapes=[pltpu.SemaphoreType.DMA],
             compiler_params=params,
             name="give",
-        )(core, place, slot, pattern, strips)
+        )(core, numbers, place, slot, pattern, strips)
         got = swapped(give, "row", 0)
         outgoing = pl.pallas_call(
             functools.partial(pack_kernel, items, sizes),
             out_shape=shape,
-            in_specs=[smem, smem, smem, smem, hbm, hbm],
+            in_specs=[smem, smem, smem, smem, smem, hbm, hbm],
             out_specs=vmem,
             scratch_shapes=[pltpu.SemaphoreType.DMA],
             compiler_params=params,
             name="pack",
-        )(core, place, slot, pattern, strips, got)
+        )(core, numbers, place, slot, pattern, strips, got)
         outgoing = outgoing.reshape(devices, slots, piece, width)
         held = lax.all_to_all(outgoing, "row", split_axis=0, concat_axis=0, tiled=True)
         return pl.pallas_call(
@@ -269,7 +268,7 @@
     outgoing = lax.switch(
         level,
         [functools.partial(hop, slots) for slots in levels],
-        strips, core, chip, place, slot, parent_pattern,
+        strips, core, numbers, chip, place, slot, parent_pattern,
     )
     arrived = lax.all_to_all(outgoing, "row", split_axis=0, concat_axis=0, tiled=True)
     return arrived.reshape(groups, struct, struct, halves * cores, piece, width)

time: 189 us -> 182 us (0.963)
  Pallas kernels: 33.7 us -> 27.4 us
    pallas_call x1, Pallas kernels: 13.8 us -> 9.71 us  [children_solve(): pl.pallas_call(child_kernel, grid_spec=pltpu.PrefetchScalarGridSpec(num_s...]
where the time goes in v1:
time: 182 us
  blocking collectives  135 us (74%)
  Pallas kernels  27.4 us (15%)
  waiting for transfers between devices  7.39 us (4%)
  local copies, waits for them, and re-layouts  4.58 us (3%)
  other arithmetic  3.2 us (2%)
  between operations  2.68 us (1%)
    all_to_all x1, blocking collectives, hop(): lax.all_to_all(outgoing, 'row', split_axis=0, concat_axis=0, tiled=True)  83.6 us
    all_to_all x1, blocking collectives, exchange_two_hops(): lax.all_to_all(outgoing, 'row', split_axis=0, concat_axis=0, tiled=True)  51.6 us
    pallas_call x1, Pallas kernels, children_solve(): pl.pallas_call(child_kernel, grid_spec=pltpu.PrefetchScalarGridSpec(num_s...  9.71 us
    ppermute x3, waiting for transfers between devices, swapped(): return lax.ppermute(value, axis, pairs)  7.39 us
    pallas_call x1, Pallas kernels, hop(): pl.pallas_call(functools.partial(give_kernel, items, sizes), out_shape=sh...  7.09 us
    pallas_call x1, Pallas kernels, hop(): pl.pallas_call(functools.partial(pack_kernel, items, sizes), out_shape=sh...  4.42 us
  transfers between devices with their start and end apart: 3, of which 2 were waited for; matrix products, arithmetic and copies ran while one was open for 0% of the time, Pallas kernels for 2%

profile of v1, /device:TPU:0, one launch (start us, length us, event | category | flops | bytes accessed | tf_op | source)
XLA Modules:
  0.0 181.8 jit_solution(3896621065951170422)
XLA Ops:
  0.7 0.7 broadcast_multiply_fusion
  1.3 0.1 copy.48
  1.4 0.1 fusion.3
  1.5 0.1 fusion.2
  1.6 0.1 div.29
  1.8 0.1 sub.26
  1.9 0.1 and.35
  2.1 0.2 convert_reduce_fusion
  2.3 0.6 reduce_max.9
  3.6 0.2 fusion.4
  3.8 1.3 fusion.5
  5.7 105.3 %conditional.1 = (bf16[16,8,2,16,256]{4,3,2,1,0:T(8,128)(2,1)S(1)}) conditional(s32[]{:T(128)} %clamp.3, (s32[1]{0:T(128)}, s32[2]{0:T(128)S(1)}, s32[128]{0:T(128)S(1)}, s32[128]{0:T(128)S(1)}, s32[16,4]{0,1:T(4,128)}, /*index=5*/bf16[40,16,10240]{2,1,0:T(8,128)(2,1)}, s32[128]{0:T(128)S(1)}) %tuple.117, ...), branch_computations={%region_4.5_spmd, %region_5.6_spmd, %region_6.7_spmd, %region_7.8_... | conditional | bytes 139985536 | solution.py:268
  5.8 0.8 copy.56.pattern
  6.5 0.0 copy-start.11
  6.5 7.1 %give.22 = bf16[4,4,26,16,256]{4,3,2,1,0:T(8,128)(2,1)S(1)} custom-call(s32[1]{0:T(128)} %get-tuple-element.277.core, s32[2]{0:T(128)S(1)} %get-tuple-element.278.numbers, s32[128]{0:T(128)S(1)} %get-tuple-element.279.place, s32[128]{0:T(128)S(1)} %get-tuple-element.276.slot, s32[16,4]{1,0:T(8,128)S(1)} %copy.56.pattern, ...), custom_call_target="tpu_custom_call" | custom-call | tf_op jit(solution)/shard_map/cond/branch_7_fun/give/pallas_call | solution.py:236
  13.6 0.4 collective-permute-start.7
  14.0 5.7 %collective-permute-done.7.got = bf16[4,4,26,16,256]{4,3,2,1,0:T(8,128)(2,1)S(1)} collective-permute-done((bf16[4,4,26,16,256]{4,3,2,1,0:T(8,128)(2,1)S(1)}, bf16[4,4,26,16,256]{4,3,2,1,0:T(8,128)(2,1)S(1)}, u32[]{:S(2)}, u32[]{:S(2)}) %collective-permute-start.7) | collective-permute-done | bytes 3407904 | tf_op jit(solution)/shard_map/cond/branch_7_fun/ppermute | solution.py:19
  19.7 0.0 copy-done.11
  19.7 4.4 %pack.22 = bf16[4,4,26,16,256]{4,3,2,1,0:T(8,128)(2,1)S(1)} custom-call(s32[1]{0:T(128)} %get-tuple-element.277.core, s32[2]{0:T(128)S(1)} %get-tuple-element.278.numbers, s32[128]{0:T(128)S(1)} %get-tuple-element.279.place, s32[128]{0:T(128)S(1)} %get-tuple-element.276.slot, s32[16,4]{1,0:T(8,128)S(1)} %copy.56.pattern, ...), custom_call_target="tpu_custom_call" | custom-call | tf_op jit(solution)/shard_map/cond/branch_7_fun/pack/pallas_call | solution.py:246
  24.1 83.6 %all_to_all.72.held = bf16[16,26,16,256]{3,2,1,0:T(8,128)(2,1)} all-to-all(bf16[16,26,16,256]{3,2,1,0:T(8,128)(2,1)S(1)} %bitcast.24), channel_id=1, replica_groups=mesh['hyper'=2,'row'=16] {'row'}, dimensions={0} | all-to-all | bytes 6815744 | tf_op jit(solution)/shard_map/cond/branch_7_fun/all_to_all | solution.py:256
  107.8 3.2 %pick.22 = bf16[16,8,2,16,256]{4,3,2,1,0:T(8,128)(2,1)S(1)} custom-call(s32[128]{0:T(128)S(1)} %get-tuple-element.275.chip, s32[128]{0:T(128)S(1)} %get-tuple-element.276.slot, bf16[16,26,16,256]{3,2,1,0:T(8,128)(2,1)} %all_to_all.72.held), custom_call_target="tpu_custom_call" | custom-call | tf_op jit(solution)/shard_map/cond/branch_7_fun/pick/pallas_call | solution.py:257
  111.1 0.0 copy-start.16
  111.1 1.3 copy-done.16
  112.4 0.0 copy-start.3
  112.4 0.0 copy-start.2
  112.4 0.0 copy-start.17
  112.4 0.0 copy-start.1
  112.4 51.6 %all_to_all.80 = bf16[16,8,2,16,256]{4,3,2,1,0:T(8,128)(2,1)S(1)} all-to-all(bf16[16,8,2,16,256]{4,3,2,1,0:T(8,128)(2,1)} %copy-done.16), channel_id=1, replica_groups=mesh['hyper'=2,'row'=16] {'row'}, dimensions={0} | all-to-all | bytes 4194304 | tf_op jit(solution)/shard_map/all_to_all | solution.py:273
  164.0 0.8 collective-permute-start.15
  164.8 0.0 copy-done.3
  164.8 0.0 copy-done.2
  164.8 2.9 %parent.1 = (bf16[1,1024,256]{2,1,0:T(8,128)(2,1)}, f32[1,256,256]{2,1,0:T(8,128)}, bf16[5,256,256]{2,1,0:T(8,128)(2,1)}) custom-call(bf16[4,4,4,4,16,256]{5,4,3,2,1,0:T(8,128)(2,1)S(1)} %bitcast.33, bf16[1,1024,256]{2,1,0:T(8,128)(2,1)S(1)} %copy-done.2, bf16[1,256,256]{2,1,0:T(8,128)(2,1)S(1)} %copy-done.3), custom_call_target="tpu_custom_call" | custom-call | tf_op jit(solution)/shard_map/parent/pallas_call | solution.py:145
  167.7 0.0 collective-permute-start.16
  167.7 0.0 copy-done.17
  167.7 0.1 copy.64.positions
  168.4 1.7 collective-permute-done.16.both
  170.1 0.0 collective-permute-done.15.raw
  170.1 0.0 copy-done.1
  170.2 0.0 copy-start
  170.2 1.9 %copy-done = bf16[8,768,256]{2,1,0:T(8,128)(2,1)S(1)} copy-done((bf16[8,768,256]{2,1,0:T(8,128)(2,1)S(1)}, bf16[8,768,256]{2,1,0:T(8,128)(2,1)}, u32[]{:S(2)}) %copy-start) | copy-done | bytes 3145752
  172.0 9.7 %children.1 = (bf16[8,768,256]{2,1,0:T(8,128)(2,1)}, f32[8,256,256]{2,1,0:T(8,128)}) custom-call(s32[8,2]{1,0:T(8,128)S(1)} %copy.64.positions, s32[1]{0:T(128)S(6)} %copy.80.count, bf16[4,4,4,4,16,256]{5,4,3,2,1,0:T(8,128)(2,1)} %collective-permute-done.15.raw, bf16[5,256,256]{2,1,0:T(8,128)(2,1)} %collective-permute-done.16.both, ...), custom_call_target="tpu_custom_call" | custom-call | tf_op jit(solution)/shard_map/children/pallas_call | solution.py:167
  (2 shorter events, 0.0 us)
Async XLA Ops:
  6.5 13.2 %copy-start.11 = (bf16[40,16,10240]{2,1,0:T(8,128)(2,1)S(1)}, bf16[40,16,10240]{2,1,0:T(8,128)(2,1)}, u32[]{:S(2)}) copy-start(bf16[40,16,10240]{2,1,0:T(8,128)(2,1)} %get-tuple-element.281.top) | copy-start | bytes 39321604 | tf_op jit(solution)/shard_map/cond
  13.6 6.1 %collective-permute-start.7 = (bf16[4,4,26,16,256]{4,3,2,1,0:T(8,128)(2,1)S(1)}, bf16[4,4,26,16,256]{4,3,2,1,0:T(8,128)(2,1)S(1)}, u32[]{:S(2)}, u32[]{:S(2)}) collective-permute-start(bf16[4,4,26,16,256]{4,3,2,1,0:T(8,128)(2,1)S(1)} %give.22), channel_id=1, source_target_pairs={{0,1},{1,0},{2,3},{3,2},{4,5},{5,4},{6,7},{7,6},{8,9},{9,8},{10,11... | collective-permute-start | bytes 10223624 | tf_op jit(solution)/shard_map/cond/branch_7_fun/ppermute | solution.py:19
  111.1 1.3 copy-start.16
  112.4 52.4 %copy-start.3 = (bf16[1,256,256]{2,1,0:T(8,128)(2,1)S(1)}, bf16[1,256,256]{2,1,0:T(8,128)(2,1)}, u32[]{:S(2)}) copy-start(bf16[1,256,256]{2,1,0:T(8,128)(2,1)} %inverse.2) | copy-start | bytes 393220
  112.4 52.4 %copy-start.2 = (bf16[1,1024,256]{2,1,0:T(8,128)(2,1)S(1)}, bf16[1,1024,256]{2,1,0:T(8,128)(2,1)}, u32[]{:S(2)}) copy-start(bf16[1,1024,256]{2,1,0:T(8,128)(2,1)} %panel.2) | copy-start | bytes 1572868
  112.4 55.3 %copy-start.17 = (s32[8,2]{0,1:T(2,128)S(1)}, s32[8,2]{0,1:T(2,128)}, u32[]{:S(2)}) copy-start(s32[8,2]{0,1:T(2,128)} %param.29) | copy-start | bytes 196
  112.4 57.8 %copy-start.1 = (bf16[8,256,256]{2,1,0:T(8,128)(2,1)S(1)}, bf16[8,256,256]{2,1,0:T(8,128)(2,1)}, u32[]{:S(2)}) copy-start(bf16[8,256,256]{2,1,0:T(8,128)(2,1)} %inverse.3) | copy-start | bytes 3145732
  164.0 6.1 %collective-permute-start.15 = (bf16[4,4,4,4,16,256]{5,4,3,2,1,0:T(8,128)(2,1)S(1)}, bf16[4,4,4,4,16,256]{5,4,3,2,1,0:T(8,128)(2,1)}, u32[]{:S(2)}, u32[]{:S(2)}) collective-permute-start(bf16[4,4,4,4,16,256]{5,4,3,2,1,0:T(8,128)(2,1)S(1)} %bitcast.32), channel_id=1, source_target_pairs={{0,1},{1,0},{2,3},{3,2},{4,5},{5,4},{6,7},{7,6},{8,9},{9,8},{10,11... | collective-permute-start | bytes 6291464 | tf_op jit(solution)/shard_map/ppermute | solution.py:19
  167.7 2.4 %collective-permute-start.16 = (bf16[5,256,256]{2,1,0:T(8,128)(2,1)}, bf16[5,256,256]{2,1,0:T(8,128)(2,1)}, u32[]{:S(2)}, u32[]{:S(2)}) collective-permute-start(bf16[5,256,256]{2,1,0:T(8,128)(2,1)} %get-tuple-element.342), channel_id=1, source_target_pairs={{0,1},{1,0},{2,3},{3,2},{4,5},{5,4},{6,7},{7,6},{8,9},{9,8},{10,11... | collective-permute-start | bytes 1966088 | tf_op jit(solution)/shard_map/ppermute | solution.py:19
  170.2 1.9 %copy-start = (bf16[8,768,256]{2,1,0:T(8,128)(2,1)S(1)}, bf16[8,768,256]{2,1,0:T(8,128)(2,1)}, u32[]{:S(2)}) copy-start(bf16[8,768,256]{2,1,0:T(8,128)(2,1)} %panel.3) | copy-start | bytes 9437188

commit v2 on v1

--- a/solution.py
+++ b/solution.py
@@ -46,7 +46,7 @@
 
 
 def give_kernel(items, sizes, core, numbers, place, slot, pattern, top, out, sem):
-    @pl.loop(0, items)
+    @pl.loop(0, items, unroll=8)
     def _(item):
         @pl.when(place[item] >= 0)
         def _():
@@ -57,7 +57,7 @@
 
 
 def pack_kernel(items, sizes, core, numbers, place, slot, pattern, top, got, out, sem):
-    @pl.loop(0, items)
+    @pl.loop(0, items, unroll=8)
     def _(item):
         @pl.when(place[item] >= 0)
         def _():
@@ -72,7 +72,7 @@
 
 
 def pick_kernel(items, per_parent, cores, chip, slot, held, out, sem):
-    @pl.loop(0, items)
+    @pl.loop(0, items, unroll=8)
     def _(item):
         for core in range(cores):
             pltpu.make_async_copy(

time: 182 us -> 175 us (0.962)
  blocking collectives: 135 us -> 129 us
    all_to_all x1, blocking collectives: 83.6 us -> 76.2 us  [hop(): lax.all_to_all(outgoing, 'row', split_axis=0, concat_axis=0, tiled=True)]
where the time goes in v2:
time: 175 us; the launch traced here: 174 us
  blocking collectives  129 us (74%)
  Pallas kernels  26.6 us (15%)
  waiting for transfers between devices  7.25 us (4%)
  local copies, waits for them, and re-layouts  4.58 us (3%)
  other arithmetic  3.2 us (2%)
  between operations  2.68 us (2%)
    all_to_all x1, blocking collectives, hop(): lax.all_to_all(outgoing, 'row', split_axis=0, concat_axis=0, tiled=True)  76.2 us
    all_to_all x1, blocking collectives, exchange_two_hops(): lax.all_to_all(outgoing, 'row', split_axis=0, concat_axis=0, tiled=True)  52.6 us
    pallas_call x1, Pallas kernels, children_solve(): pl.pallas_call(child_kernel, grid_spec=pltpu.PrefetchScalarGridSpec(num_s...  9.71 us
    ppermute x3, waiting for transfers between devices, swapped(): return lax.ppermute(value, axis, pairs)  7.25 us
    pallas_call x1, Pallas kernels, hop(): pl.pallas_call(functools.partial(give_kernel, items, sizes), out_shape=sh...  7.13 us
    pallas_call x1, Pallas kernels, hop(): pl.pallas_call(functools.partial(pack_kernel, items, sizes), out_shape=sh...  4.03 us
  transfers between devices with their start and end apart: 3, of which 2 were waited for; matrix products, arithmetic and copies ran while one was open for 0% of the time, Pallas kernels for 2%

profile of v2, /device:TPU:0, one launch (start us, length us, event | category | flops | bytes accessed | tf_op | source)
XLA Modules:
  0.0 174.5 jit_solution(846770577891662432)
XLA Ops:
  0.7 0.7 broadcast_multiply_fusion
  1.3 0.1 copy.48
  1.4 0.1 fusion.3
  1.5 0.1 fusion.2
  1.6 0.1 div.29
  1.8 0.1 sub.26
  1.9 0.1 and.35
  2.1 0.2 convert_reduce_fusion
  2.3 0.6 reduce_max.9
  3.6 0.2 fusion.4
  3.8 1.3 fusion.5
  5.7 97.1 %conditional.1 = (bf16[16,8,2,16,256]{4,3,2,1,0:T(8,128)(2,1)S(1)}) conditional(s32[]{:T(128)} %clamp.3, (s32[1]{0:T(128)}, s32[2]{0:T(128)S(1)}, s32[128]{0:T(128)S(1)}, s32[128]{0:T(128)S(1)}, s32[16,4]{0,1:T(4,128)}, /*index=5*/bf16[40,16,10240]{2,1,0:T(8,128)(2,1)}, s32[128]{0:T(128)S(1)}) %tuple.117, ...), branch_computations={%region_4.5_spmd, %region_5.6_spmd, %region_6.7_spmd, %region_7.8_... | conditional | bytes 139985536 | solution.py:268
  5.8 0.8 copy.54.pattern
  6.5 0.0 copy-start.9
  6.5 7.1 %give.20 = bf16[4,4,24,16,256]{4,3,2,1,0:T(8,128)(2,1)S(1)} custom-call(s32[1]{0:T(128)} %get-tuple-element.263.core, s32[2]{0:T(128)S(1)} %get-tuple-element.264.numbers, s32[128]{0:T(128)S(1)} %get-tuple-element.265.place, s32[128]{0:T(128)S(1)} %get-tuple-element.262.slot, s32[16,4]{1,0:T(8,128)S(1)} %copy.54.pattern, ...), custom_call_target="tpu_custom_call" | custom-call | tf_op jit(solution)/shard_map/cond/branch_5_fun/give/pallas_call | solution.py:236
  13.7 0.2 collective-permute-start.5
  13.8 5.5 %collective-permute-done.5.got = bf16[4,4,24,16,256]{4,3,2,1,0:T(8,128)(2,1)S(1)} collective-permute-done((bf16[4,4,24,16,256]{4,3,2,1,0:T(8,128)(2,1)S(1)}, bf16[4,4,24,16,256]{4,3,2,1,0:T(8,128)(2,1)S(1)}, u32[]{:S(2)}, u32[]{:S(2)}) %collective-permute-start.5) | collective-permute-done | bytes 3145760 | tf_op jit(solution)/shard_map/cond/branch_5_fun/ppermute | solution.py:19
  19.4 0.0 copy-done.9
  19.4 4.0 %pack.20 = bf16[4,4,24,16,256]{4,3,2,1,0:T(8,128)(2,1)S(1)} custom-call(s32[1]{0:T(128)} %get-tuple-element.263.core, s32[2]{0:T(128)S(1)} %get-tuple-element.264.numbers, s32[128]{0:T(128)S(1)} %get-tuple-element.265.place, s32[128]{0:T(128)S(1)} %get-tuple-element.262.slot, s32[16,4]{1,0:T(8,128)S(1)} %copy.54.pattern, ...), custom_call_target="tpu_custom_call" | custom-call | tf_op jit(solution)/shard_map/cond/branch_5_fun/pack/pallas_call | solution.py:246
  23.4 76.2 %all_to_all.70.held = bf16[16,24,16,256]{3,2,1,0:T(8,128)(2,1)} all-to-all(bf16[16,24,16,256]{3,2,1,0:T(8,128)(2,1)S(1)} %bitcast.26), channel_id=1, replica_groups=mesh['hyper'=2,'row'=16] {'row'}, dimensions={0} | all-to-all | bytes 6291456 | tf_op jit(solution)/shard_map/cond/branch_5_fun/all_to_all | solution.py:256
  99.6 2.9 %pick.20 = bf16[16,8,2,16,256]{4,3,2,1,0:T(8,128)(2,1)S(1)} custom-call(s32[128]{0:T(128)S(1)} %get-tuple-element.261.chip, s32[128]{0:T(128)S(1)} %get-tuple-element.262.slot, bf16[16,24,16,256]{3,2,1,0:T(8,128)(2,1)} %all_to_all.70.held), custom_call_target="tpu_custom_call" | custom-call | tf_op jit(solution)/shard_map/cond/branch_5_fun/pick/pallas_call | solution.py:257
  102.8 0.0 copy-start.16
  102.8 1.3 copy-done.16
  104.1 0.0 copy-start.3
  104.1 0.0 copy-start.2
  104.1 0.0 copy-start.17
  104.1 0.0 copy-start.1
  104.1 52.6 %all_to_all.80 = bf16[16,8,2,16,256]{4,3,2,1,0:T(8,128)(2,1)S(1)} all-to-all(bf16[16,8,2,16,256]{4,3,2,1,0:T(8,128)(2,1)} %copy-done.16), channel_id=1, replica_groups=mesh['hyper'=2,'row'=16] {'row'}, dimensions={0} | all-to-all | bytes 4194304 | tf_op jit(solution)/shard_map/all_to_all | solution.py:273
  156.8 0.8 collective-permute-start.15
  157.5 0.0 copy-done.3
  157.5 0.0 copy-done.2
  157.5 2.9 %parent.1 = (bf16[1,1024,256]{2,1,0:T(8,128)(2,1)}, f32[1,256,256]{2,1,0:T(8,128)}, bf16[5,256,256]{2,1,0:T(8,128)(2,1)}) custom-call(bf16[4,4,4,4,16,256]{5,4,3,2,1,0:T(8,128)(2,1)S(1)} %bitcast.33, bf16[1,1024,256]{2,1,0:T(8,128)(2,1)S(1)} %copy-done.2, bf16[1,256,256]{2,1,0:T(8,128)(2,1)S(1)} %copy-done.3), custom_call_target="tpu_custom_call" | custom-call | tf_op jit(solution)/shard_map/parent/pallas_call | solution.py:145
  160.4 0.0 collective-permute-start.16
  160.4 0.0 copy-done.17
  160.5 0.1 copy.64.positions
  161.2 1.7 collective-permute-done.16.both
  162.9 0.0 collective-permute-done.15.raw
  162.9 0.0 copy-done.1
  162.9 0.0 copy-start
  162.9 1.9 %copy-done = bf16[8,768,256]{2,1,0:T(8,128)(2,1)S(1)} copy-done((bf16[8,768,256]{2,1,0:T(8,128)(2,1)S(1)}, bf16[8,768,256]{2,1,0:T(8,128)(2,1)}, u32[]{:S(2)}) %copy-start) | copy-done | bytes 3145752
  164.8 9.7 %children.1 = (bf16[8,768,256]{2,1,0:T(8,128)(2,1)}, f32[8,256,256]{2,1,0:T(8,128)}) custom-call(s32[8,2]{1,0:T(8,128)S(1)} %copy.64.positions, s32[1]{0:T(128)S(6)} %copy.80.count, bf16[4,4,4,4,16,256]{5,4,3,2,1,0:T(8,128)(2,1)} %collective-permute-done.15.raw, bf16[5,256,256]{2,1,0:T(8,128)(2,1)} %collective-permute-done.16.both, ...), custom_call_target="tpu_custom_call" | custom-call | tf_op jit(solution)/shard_map/children/pallas_call | solution.py:167
  (2 shorter events, 0.0 us)
Async XLA Ops:
  6.5 12.9 %copy-start.9 = (bf16[40,16,10240]{2,1,0:T(8,128)(2,1)S(1)}, bf16[40,16,10240]{2,1,0:T(8,128)(2,1)}, u32[]{:S(2)}) copy-start(bf16[40,16,10240]{2,1,0:T(8,128)(2,1)} %get-tuple-element.267.top) | copy-start | bytes 39321604 | tf_op jit(solution)/shard_map/cond
  13.7 5.7 %collective-permute-start.5 = (bf16[4,4,24,16,256]{4,3,2,1,0:T(8,128)(2,1)S(1)}, bf16[4,4,24,16,256]{4,3,2,1,0:T(8,128)(2,1)S(1)}, u32[]{:S(2)}, u32[]{:S(2)}) collective-permute-start(bf16[4,4,24,16,256]{4,3,2,1,0:T(8,128)(2,1)S(1)} %give.20), channel_id=1, source_target_pairs={{0,1},{1,0},{2,3},{3,2},{4,5},{5,4},{6,7},{7,6},{8,9},{9,8},{10,11... | collective-permute-start | bytes 9437192 | tf_op jit(solution)/shard_map/cond/branch_5_fun/ppermute | solution.py:19
  102.8 1.3 copy-start.16
  104.1 53.4 %copy-start.3 = (bf16[1,256,256]{2,1,0:T(8,128)(2,1)S(1)}, bf16[1,256,256]{2,1,0:T(8,128)(2,1)}, u32[]{:S(2)}) copy-start(bf16[1,256,256]{2,1,0:T(8,128)(2,1)} %inverse.2) | copy-start | bytes 393220
  104.1 53.4 %copy-start.2 = (bf16[1,1024,256]{2,1,0:T(8,128)(2,1)S(1)}, bf16[1,1024,256]{2,1,0:T(8,128)(2,1)}, u32[]{:S(2)}) copy-start(bf16[1,1024,256]{2,1,0:T(8,128)(2,1)} %panel.2) | copy-start | bytes 1572868
  104.1 56.3 %copy-start.17 = (s32[8,2]{0,1:T(2,128)S(1)}, s32[8,2]{0,1:T(2,128)}, u32[]{:S(2)}) copy-start(s32[8,2]{0,1:T(2,128)} %param.29) | copy-start | bytes 196
  104.1 58.8 %copy-start.1 = (bf16[8,256,256]{2,1,0:T(8,128)(2,1)S(1)}, bf16[8,256,256]{2,1,0:T(8,128)(2,1)}, u32[]{:S(2)}) copy-start(bf16[8,256,256]{2,1,0:T(8,128)(2,1)} %inverse.3) | copy-start | bytes 3145732
  156.8 6.1 %collective-permute-start.15 = (bf16[4,4,4,4,16,256]{5,4,3,2,1,0:T(8,128)(2,1)S(1)}, bf16[4,4,4,4,16,256]{5,4,3,2,1,0:T(8,128)(2,1)}, u32[]{:S(2)}, u32[]{:S(2)}) collective-permute-start(bf16[4,4,4,4,16,256]{5,4,3,2,1,0:T(8,128)(2,1)S(1)} %bitcast.32), channel_id=1, source_target_pairs={{0,1},{1,0},{2,3},{3,2},{4,5},{5,4},{6,7},{7,6},{8,9},{9,8},{10,11... | collective-permute-start | bytes 6291464 | tf_op jit(solution)/shard_map/ppermute | solution.py:19
  160.4 2.4 %collective-permute-start.16 = (bf16[5,256,256]{2,1,0:T(8,128)(2,1)}, bf16[5,256,256]{2,1,0:T(8,128)(2,1)}, u32[]{:S(2)}, u32[]{:S(2)}) collective-permute-start(bf16[5,256,256]{2,1,0:T(8,128)(2,1)} %get-tuple-element.342), channel_id=1, source_target_pairs={{0,1},{1,0},{2,3},{3,2},{4,5},{5,4},{6,7},{7,6},{8,9},{9,8},{10,11... | collective-permute-start | bytes 1966088 | tf_op jit(solution)/shard_map/ppermute | solution.py:19
  162.9 1.9 %copy-start = (bf16[8,768,256]{2,1,0:T(8,128)(2,1)S(1)}, bf16[8,768,256]{2,1,0:T(8,128)(2,1)}, u32[]{:S(2)}) copy-start(bf16[8,768,256]{2,1,0:T(8,128)(2,1)} %panel.3) | copy-start | bytes 9437188
